TPU v7x, 128 devices: a whole 4x4x4 slice. The times are simulated.
128 devices in a mesh: member: 16 (over y, x_lo, core), tp: 8 (over x_hi, z).
Axes of the slice: x: 4 (x_hi: 2, x_lo: 2; x = x_hi * 2 + x_lo), y: 4, z: 4, core: 2. Of those that a mesh axis runs over, the one named last changes fastest.
Arguments:
- acts: bfloat16 [16, 512, 2560], P('member', None, 'tp'), may hold values from -8 to 8
- weights: bfloat16 [16, 2560, 1024], P('member', 'tp'), may hold values from -6 to 6
Outputs:
- merged: bfloat16 [2560, 1024], P(None, 'tp')
All inputs are finite; a program needn't handle non-finite values.
Results may differ from a plain program's by a relative error of at most 0.005.
Values may be sent and summed in bfloat16 or wider, within the bound.
A program may use at most 256 MiB of HBM per device.

v0:
```python
import jax
import jax.numpy as jnp
from jax import lax
from jax.sharding import PartitionSpec as P

shrink = 0.9
block_rows = 512


def block_cholesky(matrix):
    total = matrix.shape[0]
    trailing = matrix
    columns = []
    start = 0
    while start < total:
        width = min(block_rows, total - start)
        diag_block = jnp.linalg.cholesky(trailing[:width, :width])
        if width < trailing.shape[0]:
            below = jax.scipy.linalg.solve_triangular(
                diag_block, trailing[width:, :width].T, lower=True
            ).T
            column = jnp.concatenate([diag_block, below], 0)
            trailing = trailing[width:, width:] - jnp.dot(
                below, below.T, precision=lax.Precision.HIGHEST
            )
        else:
            column = diag_block
        columns.append(jnp.pad(column, ((start, 0), (0, 0))))
        start = start + width
    return jnp.concatenate(columns, 1)


def block_solve(factor, right):
    total = factor.shape[0]
    bounds = []
    start = 0
    while start < total:
        width = min(block_rows, total - start)
        bounds.append((start, start + width))
        start = start + width
    forward = []
    for first, last in bounds:
        rhs_part = right[first:last]
        if first > 0:
            earlier = jnp.concatenate(forward, 0)
            rhs_part = rhs_part - jnp.dot(
                factor[first:last, :first], earlier, precision=lax.Precision.HIGHEST
            )
        forward.append(
            jax.scipy.linalg.solve_triangular(factor[first:last, first:last], rhs_part, lower=True)
        )
    backward = [None] * len(bounds)
    for index in range(len(bounds) - 1, -1, -1):
        first, last = bounds[index]
        rhs_part = forward[index]
        if last < total:
            later = jnp.concatenate(backward[index + 1 :], 0)
            rhs_part = rhs_part - jnp.dot(
                factor[last:, first:last].T, later, precision=lax.Precision.HIGHEST
            )
        backward[index] = jax.scipy.linalg.solve_triangular(
            factor[first:last, first:last], rhs_part, lower=True, trans=1
        )
    return jnp.concatenate(backward, 0)


def local(acts, weights):
    own_acts = acts[0]
    own_weight = weights[0]
    row_count = own_acts.shape[0]
    own_width = own_acts.shape[1]
    tp_count = lax.axis_size("tp")
    member_count = lax.axis_size("member")
    total_width = own_width * tp_count
    col_total = own_weight.shape[1]
    col_block = col_total // (member_count * tp_count)
    gathered = lax.all_gather(own_acts, "tp", axis=1, tiled=True)
    own_diag = jnp.sum(jnp.square(own_acts.astype(jnp.float32)), axis=0)
    partial_prod = jnp.dot(own_acts, own_weight, preferred_element_type=jnp.float32)
    reduced = lax.psum(partial_prod, "tp").astype(jnp.bfloat16)
    reduced_split = reduced.reshape(row_count, tp_count, member_count, col_block)
    weight_split = own_weight.reshape(own_width, tp_count, member_count, col_block)
    block_count = own_width * lax.axis_size("member") // own_width
    contrib = shrink * jnp.einsum(
        "rf,rsjc->jfsc", own_acts, reduced_split, preferred_element_type=jnp.float32
    )
    scaled = own_diag[None, :, None, None] * weight_split.transpose(2, 0, 1, 3).astype(jnp.float32)
    contrib = contrib + (1.0 - shrink) * scaled
    right_rows = lax.psum_scatter(
        contrib.reshape(block_count * own_width, tp_count * col_block),
        "member",
        scatter_dimension=0,
        tiled=True,
    )
    right_cols = lax.all_to_all(right_rows, "tp", split_axis=1, concat_axis=0, tiled=True)
    share_rows = own_width // member_count
    gram_share = lax.psum_scatter(
        jnp.dot(own_acts.T, gathered, preferred_element_type=jnp.float32),
        "member",
        scatter_dimension=0,
        tiled=True,
    )
    gathered_gram = lax.all_gather(gram_share, ("member", "tp"), axis=0, tiled=True)
    gram_total = gathered_gram.reshape(member_count, tp_count, share_rows, total_width)
    gram_total = gram_total.transpose(1, 0, 2, 3).reshape(total_width, total_width)
    on_diagonal = jnp.eye(total_width, dtype=bool)
    merged_gram = jnp.where(on_diagonal, gram_total, shrink * gram_total)
    factor = block_cholesky(merged_gram)
    solution = block_solve(factor, right_cols).astype(jnp.bfloat16)
    return lax.all_gather(solution, "member", axis=1, tiled=True)


def solution(mesh):
    in_specs = (P("member", None, "tp"), P("member", "tp", None))
    out_specs = P(None, "tp")
    return jax.shard_map(local, mesh=mesh, in_specs=in_specs, out_specs=out_specs, check_vma=False)
```

profile of v0, /device:TPU:1, one launch (start us, length us, event | category | flops | bytes accessed | tf_op | source)
XLA Modules:
  0.0 1624.9 jit_solution(12626059798473018231)
XLA Ops:
  12.6 82.7 %all-reduce.7 = bf16[512,1024]{1,0:T(8,128)(2,1)S(1)} all-reduce(f32[512,1024]{1,0:T(8,128)S(1)} %fusion.68), channel_id=1, replica_groups=mesh['member'=16,'tp'=8] {'tp'}, use_global_device_ids=true, to_apply=%region_9.11 | all-reduce | flops 524288 | bytes 3145728 | tf_op jit(solution)/shard_map/psum | solution.py:80
  104.9 82.4 %fusion = f32[24,2560]{1,0:T(8,128)S(1)} fusion(f32[320,2560]{1,0:T(8,128)S(1)} %fusion.11), kind=kCustom, calls=%all-reduce-scatter | all-reduce-scatter fusion | flops 983041 | bytes 3523072
  220.2 333.8 %all-gather.7.cloned.1.call-done = f32[128,20,2560]{2,1,0:T(8,128)} async-done(((f32[1,20,2560]{2,1,0:T(8,128)}), f32[128,20,2560]{2,1,0:T(8,128)}) %all-gather.7.cloned.1.call-update) | async-done | bytes 26214416 | tf_op jit(solution)/shard_map/all_gather | solution.py:103
  553.9 21.5 %copy.110 = f32[16,8,20,2560]{3,2,0,1:T(8,128)} copy(f32[16,8,20,2560]{3,2,1,0:T(8,128)} %bitcast.436) | data formatting | bytes 52428800 | tf_op jit(solution)/shard_map/reshape | solution.py:104
  575.5 27.5 %reshape.106 = f32[2560,2560]{1,0:T(8,128)} reshape(f32[8,16,20,2560]{3,2,1,0:T(8,128)} %bitcast.435) | data formatting | bytes 52428800 | tf_op jit(solution)/shard_map/reshape | solution.py:105
  603.0 27.3 %copy.67 = f32[2560,2560]{0,1:T(8,128)} copy(f32[2560,2560]{1,0:T(8,128)} %reshape.106) | data formatting | bytes 52428800 | tf_op jit(solution)/shard_map/reshape | solution.py:105
  654.0 11.7 cholesky.550
  676.4 11.7 cholesky.569
  699.0 11.7 cholesky.590
  721.8 11.9 cholesky.607
  745.5 39.3 %custom-call.90 = f32[4,128,128]{1,2,0:T(8,128)S(1)} custom-call(f32[4,128,128]{2,1,0:T(8,128)S(1)} %get-tuple-element.113), custom_call_target="InvertDiagBlocksLowerTriangular" | custom-call | tf_op jit(solution)/shard_map/jit(_solve_triangular)/triangular_solve | solution.py:61
  811.3 30.2 %slice_subtract_fusion = f32[2048,2048]{0,1:T(8,128)S(1)} fusion(f32[2560,2560]{0,1:T(8,128)} %copy-done, f32[128,2048]{0,1:T(8,128)S(1)} %fusion.259, f32[128,2048]{0,1:T(8,128)S(1)} %copy-done.13, f32[128,2048]{0,1:T(8,128)S(1)} %copy-done.15, f32[128,2048]{0,1:T(8,128)S(1)} %copy-done.17), kind=kOutput, calls=%fused_computation.13 | convolution fusion | flops 25777143808 | bytes 37748736 | tf_op jit(solution)/shard_map/dot_general | solution.py:23
  919.8 11.9 cholesky.679
  943.9 39.3 %custom-call.89 = f32[4,128,128]{1,2,0:T(8,128)S(1)} custom-call(f32[4,128,128]{2,1,0:T(8,128)S(1)} %get-tuple-element.112), custom_call_target="InvertDiagBlocksLowerTriangular" | custom-call | tf_op jit(solution)/shard_map/jit(_solve_triangular)/triangular_solve | solution.py:61
  1006.0 19.4 %slice_subtract_fusion.1 = f32[1536,1536]{0,1:T(8,128)S(1)} fusion(f32[2048,2048]{0,1:T(8,128)} %copy-done.4, f32[128,1536]{0,1:T(8,128)S(1)} %fusion.270, f32[128,1536]{0,1:T(8,128)S(1)} %copy-done.22, f32[128,1536]{0,1:T(8,128)S(1)} %copy-done.23, f32[128,1536]{0,1:T(8,128)S(1)} %copy-done.25), kind=kOutput, calls=%fused_computation.14 | convolution fusion | flops 14500233216 | bytes 22020096 | tf_op jit(solution)/shard_map/dot_general | solution.py:23
  1107.5 12.1 cholesky.751
  1135.5 39.3 %custom-call.88 = f32[4,128,128]{1,2,0:T(8,128)S(1)} custom-call(f32[4,128,128]{2,1,0:T(8,128)S(1)} %get-tuple-element.111), custom_call_target="InvertDiagBlocksLowerTriangular" | custom-call | tf_op jit(solution)/shard_map/jit(_solve_triangular)/triangular_solve | solution.py:61
  1261.3 13.2 cholesky.806
  1290.2 11.9 cholesky.823
  1318.4 39.3 %custom-call.87 = f32[4,128,128]{1,2,0:T(8,128)S(1)} custom-call(f32[4,128,128]{2,1,0:T(8,128)S(1)} %get-tuple-element.110), custom_call_target="InvertDiagBlocksLowerTriangular" | custom-call | tf_op jit(solution)/shard_map/jit(_solve_triangular)/triangular_solve | solution.py:61
  1463.6 13.2 cholesky.878
  1492.4 11.7 cholesky.895
  1519.6 39.3 %custom-call.86 = f32[4,128,128]{1,2,0:T(8,128)S(1)} custom-call(f32[4,128,128]{2,1,0:T(8,128)S(1)} %get-tuple-element.109), custom_call_target="InvertDiagBlocksLowerTriangular" | custom-call | tf_op jit(solution)/shard_map/jit(_solve_triangular)/triangular_solve | solution.py:61
  1593.3 22.6 %all_gather.11 = bf16[2560,128]{0,1:T(8,128)(2,1)S(1)} all-gather(bf16[2560,8]{0,1:T(8,128)(2,1)S(1)} %constant_dynamic-update-slice_fusion), channel_id=1, replica_groups=mesh['member'=16,'tp'=8] {'member'}, dimensions={1}, use_global_device_ids=true | all-gather | bytes 696320 | tf_op jit(solution)/shard_map/all_gather | solution.py:110
  (558 shorter events, 678.7 us)
Async XLA Ops:
  7.4 94.6 %all-gather.5.cloned.1.call-start = ((), (), s32[]{:S(2)}) async-start(), calls=%async_computation.2 | async-start | bytes 2949120 | tf_op jit(solution)/shard_map/all_gather | solution.py:77
  8.1 198.1 %reduce-scatter.6.cloned.1.call-start = ((), (), s32[]{:S(2)}) async-start(), calls=%async_computation.4 | async-start | bytes 2785280
  12.6 84.1 %copy-start.11 = (bf16[1,512,320]{1,2,0:T(8,128)(2,1)S(1)}, bf16[1,512,320]{1,2,0:T(8,128)(2,1)}, u32[]{:S(2)}) copy-start(bf16[1,512,320]{1,2,0:T(8,128)(2,1)} %param.7) | copy-start | bytes 983044
  101.9 452.1 %all-gather.7.cloned.1.call-start = ((), (), s32[]{:S(2)}) async-start(), calls=%async_computation.3 | async-start | bytes 31703040 | tf_op jit(solution)/shard_map/all_gather | solution.py:103
  104.9 91.7 %copy-start.91 = (u32[128]{0:T(128)S(1)}, u32[128]{0:T(128)}, u32[]{:S(2)}) copy-start(u32[128]{0:T(128)} %constant.296) | copy-start | bytes 1540
  187.2 17.5 %collective-permute-start = (f32[24,2560]{1,0:T(8,128)S(1)}, f32[24,2560]{1,0:T(8,128)S(1)}, u32[]{:S(2)}, u32[]{:S(2)}) collective-permute-start(f32[24,2560]{1,0:T(8,128)S(1)} %fusion), channel_id=1, source_target_pairs={{0,8},{8,16},{16,24},{24,32},{32,40},{40,48},{48,56},{56,64},{64,7... | collective-permute-start | bytes 737288
  191.3 13.5 collective-permute-start.1
  195.1 9.7 collective-permute-start.2
  207.9 11.5 all-to-all-start
  745.5 41.8 %copy-start.32 = (f32[512,512]{1,0:T(8,128)}, f32[512,512]{1,0:T(8,128)S(1)}, u32[]{:S(2)}) copy-start(f32[512,512]{1,0:T(8,128)S(1)} %get-tuple-element.465) | copy-start | bytes 3145732
  784.8 19.1 %copy-start.46 = (f32[4,128,128]{1,2,0:T(8,128)}, f32[4,128,128]{1,2,0:T(8,128)S(1)}, u32[]{:S(2)}) copy-start(f32[4,128,128]{1,2,0:T(8,128)S(1)} %custom-call.90) | copy-start | bytes 786436
  943.9 41.5 %copy-start.31 = (f32[512,512]{1,0:T(8,128)}, f32[512,512]{1,0:T(8,128)S(1)}, u32[]{:S(2)}) copy-start(f32[512,512]{1,0:T(8,128)S(1)} %get-tuple-element.464) | copy-start | bytes 3145732
  983.2 16.7 %copy-start.48 = (f32[4,128,128]{1,2,0:T(8,128)}, f32[4,128,128]{1,2,0:T(8,128)S(1)}, u32[]{:S(2)}) copy-start(f32[4,128,128]{1,2,0:T(8,128)S(1)} %custom-call.89) | copy-start | bytes 786436
  1002.5 23.0 %copy-start.27 = (f32[128,1536]{0,1:T(8,128)}, f32[128,1536]{0,1:T(8,128)S(1)}, u32[]{:S(2)}) copy-start(f32[128,1536]{0,1:T(8,128)S(1)} %fusion.270) | copy-start | bytes 2359300
  1190.6 11.9 copy-start.38
  1366.4 15.1 copy-start.2
  1368.2 14.3 copy-start.61
  1370.3 19.7 %copy-start.9 = (f32[1536,512]{1,0:T(8,128)S(1)}, f32[1536,512]{1,0:T(8,128)}, u32[]{:S(2)}) copy-start(f32[1536,512]{1,0:T(8,128)} %fusion.70) | copy-start | bytes 9437188
  1370.3 19.7 %copy-start.41 = (f32[512,512]{1,0:T(8,128)S(1)}, f32[512,512]{1,0:T(8,128)}, u32[]{:S(2)}) copy-start(f32[512,512]{1,0:T(8,128)} %get-tuple-element.159) | copy-start | bytes 3145732
  1379.2 19.0 %copy-start.66 = (f32[128,8]{0,1:T(8,128)}, f32[128,8]{0,1:T(8,128)S(1)}, u32[]{:S(2)}) copy-start(f32[128,8]{0,1:T(8,128)S(1)} %fusion.257) | copy-start | bytes 12292
  1381.5 16.7 %copy-start.72 = (f32[128,8]{0,1:T(8,128)}, f32[128,8]{0,1:T(8,128)S(1)}, u32[]{:S(2)}) copy-start(f32[128,8]{0,1:T(8,128)S(1)} %fusion.260) | copy-start | bytes 12292
  1385.6 12.6 copy-start.68
  1387.7 10.5 copy-start.74
  1402.9 20.1 %copy-start.84 = (f32[128,8]{0,1:T(8,128)}, f32[128,8]{0,1:T(8,128)S(1)}, u32[]{:S(2)}) copy-start(f32[128,8]{0,1:T(8,128)S(1)} %fusion.287) | copy-start | bytes 12292
  (75 other events, 343.5 us)
Sparse Core Ops, SparseCore 0:
  10.5 80.5 all-gather.4
  206.3 347.6 all-gather.6
Sparse Core Ops, SparseCore 1:
  102.0 84.9 reduce-scatter.5
where the time goes:
time: 1640 us; the launch traced here: 1620 us
  other arithmetic  646 us (39%)
  waiting for transfers between devices  348 us (21%)
  matrix products  205 us (12%)
  local copies, waits for them, and re-layouts  194 us (12%)
  blocking collectives  188 us (11%)
  between operations  30.3 us (2%)
    another operation x74, other arithmetic, block_cholesky(): diag_block = jnp.linalg.cholesky(trailing[:width, :width])  408 us
    all_gather x1, waiting for transfers between devices, local(): lax.all_gather(gram_share, ('member', 'tp'), axis=0, tiled=True)  334 us
    another operation x11, other arithmetic, block_solve(): jax.scipy.linalg.solve_triangular(factor[first:last, first:last], rhs_par...  203 us
    psum x1, blocking collectives, local(): reduced = lax.psum(partial_prod, 'tp').astype(jnp.bfloat16)  82.7 us
    unnamed x1, blocking collectives  82.4 us
    dot_general x4, matrix products, block_cholesky(): jnp.dot(below, below.T, precision=lax.Precision.HIGHEST)  62.2 us
    reshape x2, local copies, waits for them, and re-layouts, local(): gram_total.transpose(1, 0, 2, 3).reshape(total_width, total_width)  54.8 us
    another operation x28, matrix products, block_cholesky(): jax.scipy.linalg.solve_triangular(diag_block, trailing[width:, :width].T,...  51.1 us
  transfers between devices with their start and end apart: 7, of which 3 were waited for; matrix products, arithmetic and copies ran while one was open for 6% of the time, Pallas kernels for 0%

commit v1 on v0

v1 whole, which is shorter than its diff:
```python
import jax
import jax.numpy as jnp
from jax import lax
from jax.experimental import pallas as pl
from jax.experimental.pallas import tpu as pltpu
from jax.sharding import PartitionSpec as P

f32, bf16 = jnp.float32, jnp.bfloat16
SHRINK = 0.9
B = 256
H = 128
NT = (((1,), (1,)), ((), ()))
NN = (((1,), (0,)), ((), ()))
TN = (((0,), (0,)), ((), ()))


def split(x):
    hi = x.astype(bf16)
    return hi, (x - hi.astype(f32)).astype(bf16)


def mm(a, b, dims=NN):
    return lax.dot_general(a, b, dims, preferred_element_type=f32)


def mm3(a, b, dims=NN):
    ah, al = split(a)
    bh, bl = split(b)
    return mm(ah, bh, dims) + (mm(ah, bl, dims) + mm(al, bh, dims))


def recip(d):
    r = pl.reciprocal(d, approx=True)
    r = r * (2.0 - d * r)
    return r * (2.0 - d * r)


def inverse_factor(block):
    groups = H // 8
    lane = lax.broadcasted_iota(jnp.int32, (8, H), 1)
    sub = lax.broadcasted_iota(jnp.int32, (8, H), 0)
    a = [block[8 * g : 8 * g + 8, :] for g in range(groups)]
    out = []
    for t in range(groups):
        base = 8 * t
        slab = a[t]
        in_block = (lane >= base) & (lane < base + 8)
        rows = [jnp.broadcast_to(slab[i : i + 1, :], (8, H)) for i in range(8)]
        e = [
            [jnp.broadcast_to(rows[i][:, base + c : base + c + 1], (8, H)) for c in range(i + 1)]
            for i in range(8)
        ]
        r = [jnp.where(in_block, (lane == base + i).astype(f32), rows[i]) for i in range(8)]
        inv = [None] * 8
        low = [[None] * 8 for _ in range(8)]
        for c in range(8):
            inv[c] = recip(e[c][c])
            for i in range(c + 1, 8):
                low[i][c] = e[i][c] * inv[c]
            for i in range(c + 1, 8):
                for j in range(c + 1, i + 1):
                    e[i][j] = e[i][j] - low[i][c] * e[j][c]
                r[i] = r[i] - low[i][c] * r[c]
        own = jnp.zeros((8, H), f32)
        for i in range(8):
            own = jnp.where(sub == i, r[i] * lax.rsqrt(e[i][i]), own)
        out.append(jnp.where(lane < base + 8, own, 0.0))
        if t + 1 < groups:
            z = [r[i] * inv[i] for i in range(8)]
            for i in range(7, 0, -1):
                for j in range(i):
                    z[j] = z[j] - low[i][j] * z[i]
            for g in range(t + 1, groups):
                new = jnp.where(in_block, 0.0, a[g])
                for j in range(8):
                    new = new - jnp.broadcast_to(a[g][:, base + j : base + j + 1], (8, H)) * z[j]
                a[g] = new
    return jnp.concatenate(out, 0)

N = 2560
NB = N // B
RC = 128


def factor_kernel(g_hbm, r_ref, o_ref, panel, low, y_low, y, x_low, w_low, acc, sems):
    def fetch(k, slot):
        cols = pl.ds(pl.multiple_of(k * B, B), B)
        return pltpu.make_async_copy(g_hbm.at[:, cols], panel.at[slot], sems.at[slot])

    fetch(0, 0).start()
    row = lax.broadcasted_iota(jnp.int32, (B, B), 0)
    col = lax.broadcasted_iota(jnp.int32, (B, B), 1)

    def step(k, _):
        slot = lax.rem(k, 2)
        fetch(k, slot).wait()

        @pl.when(k + 1 < NB)
        def _():
            fetch(k + 1, 1 - slot).start()

        own_cols = pl.ds(pl.multiple_of(k * B, B), B)

        def subtract(lhs_ref, rows, acc_rows):
            def one(j, _):
                cols = pl.ds(pl.multiple_of(j * B, B), B)
                lhs = lhs_ref[:, cols]
                both = mm(lhs, low[k, :B, cols], NT)
                cross = mm(lhs[:rows], low[k, B:, cols], NT)
                acc[acc_rows, :] = acc[acc_rows, :] - (both[:rows] + (both[rows:] + cross))
                return 0

            lax.fori_loop(0, k, one, 0)

        tile = panel[slot, own_cols, :]
        acc[...] = jnp.where(row == col, tile, SHRINK * tile)
        subtract(low.at[k], B, pl.ds(0, B))
        w1 = inverse_factor(acc[:H, :H])
        l21 = mm3(acc[H:, :H], w1, NT)
        w2 = inverse_factor(acc[H:, H:] - mm3(l21, l21, NT))
        w21 = -mm3(w2, mm3(l21, w1))
        top = jnp.concatenate([w1, jnp.zeros((H, H), f32)], 1)
        w = jnp.concatenate([top, jnp.concatenate([w21, w2], 1)], 0)
        wh, wl = split(w)
        w_low[k, :B, :] = wh
        w_low[k, B:, :] = wl

        def scale(value):
            ch, cl = split(value)
            wh = w_low[k, :B, :]
            return mm(ch, wh, NT) + (mm(ch, w_low[k, B:, :], NT) + mm(cl, wh, NT))

        def below(i, _):
            acc[...] = SHRINK * panel[slot, pl.ds(pl.multiple_of(i * B, B), B), :]
            subtract(low.at[i], B, pl.ds(0, B))
            h, l = split(scale(acc[...]))
            low[i, :B, own_cols] = h
            low[i, B:, own_cols] = l
            return 0

        lax.fori_loop(k + 1, NB, below, 0)
        acc[:RC, :] = r_ref[:, own_cols]
        subtract(y_low, RC, pl.ds(0, RC))
        yk = scale(acc[:RC, :])
        y[:, own_cols] = yk
        h, l = split(yk)
        y_low[:RC, own_cols] = h
        y_low[RC:, own_cols] = l
        return 0

    lax.fori_loop(0, NB, step, 0)

    def back(s, _):
        k = NB - 1 - s
        own_cols = pl.ds(pl.multiple_of(k * B, B), B)
        acc[:RC, :] = y[:, own_cols]

        def one(i, _):
            cols = pl.ds(pl.multiple_of(i * B, B), B)
            lhs = x_low[:, cols]
            both = mm(lhs, low[i, :B, own_cols])
            cross = mm(lhs[:RC], low[i, B:, own_cols])
            acc[:RC, :] = acc[:RC, :] - (both[:RC] + (both[RC:] + cross))
            return 0

        lax.fori_loop(k + 1, NB, one, 0)
        ch, cl = split(acc[:RC, :])
        wh = w_low[k, :B, :]
        xk = mm(ch, wh) + (mm(ch, w_low[k, B:, :]) + mm(cl, wh))
        h, l = split(xk)
        x_low[:RC, own_cols] = h
        x_low[RC:, own_cols] = l
        o_ref[own_cols, :] = xk.T.astype(bf16)
        return 0

    lax.fori_loop(0, NB, back, 0)


def factor_solve(gram, right_t):
    return pl.pallas_call(
        factor_kernel,
        out_shape=jax.ShapeDtypeStruct((N, RC), bf16),
        in_specs=[pl.BlockSpec(memory_space=pl.ANY), pl.BlockSpec(memory_space=pltpu.VMEM)],
        out_specs=pl.BlockSpec(memory_space=pltpu.VMEM),
        scratch_shapes=[
            pltpu.VMEM((2, N, B), f32),
            pltpu.VMEM((NB, 2 * B, N), bf16),
            pltpu.VMEM((2 * RC, N), bf16),
            pltpu.VMEM((RC, N), f32),
            pltpu.VMEM((2 * RC, N), bf16),
            pltpu.VMEM((NB, 2 * B, B), bf16),
            pltpu.VMEM((B, B), f32),
            pltpu.SemaphoreType.DMA((2,)),
        ],
        compiler_params=pltpu.CompilerParams(vmem_limit_bytes=56 * 1024 * 1024),
    )(gram, right_t)


def local(acts, weights):
    own = acts[0]
    gathered = lax.all_gather(own, "tp", axis=1, tiled=True)
    columns = lax.all_to_all(weights[0], "tp", split_axis=1, concat_axis=0, tiled=True)
    projected = mm(gathered, columns).astype(bf16)
    diag = jnp.sum(jnp.square(gathered.astype(f32)), axis=0)
    right_t = SHRINK * mm(projected, gathered, TN)
    right_t = right_t + (1.0 - SHRINK) * diag[None, :] * columns.T.astype(f32)
    share = lax.psum_scatter(mm(own, gathered, TN), "member", scatter_dimension=0, tiled=True)
    gram = lax.all_gather(share, ("tp", "member"), axis=0, tiled=True)
    right_t = lax.psum(right_t, "member")
    return factor_solve(gram, right_t)


def solution(mesh):
    in_specs = (P("member", None, "tp"), P("member", "tp", None))
    return jax.shard_map(
        local, mesh=mesh, in_specs=in_specs, out_specs=P(None, "tp"), check_vma=False
    )
```

time: 1640 us -> 729 us (0.44)
  other arithmetic: 646 us -> 0.59 us
  Pallas kernels: 0 us -> 227 us
  matrix products: 205 us -> 8.04 us
  local copies, waits for them, and re-layouts: 194 us -> 30.8 us
  blocking collectives: 188 us -> 64 us
  waiting for transfers between devices: 348 us -> 376 us
  between operations: 30.3 us -> 13.9 us
    another operation x85 -> x0, other arithmetic: 610 us -> none  [the longest x74 408 us: block_cholesky(): diag_block = jnp.linalg.cholesky(trailing[:width, :width])]
    pallas_call x0 -> x1, Pallas kernels: none -> 227 us  [factor_solve(): pl.pallas_call(factor_kernel, out_shape=jax.ShapeDtypeStruct((N, RC), bf1...]
    another operation x128 -> x0, matrix products: 119 us -> none  [the longest x28 51.1 us: block_cholesky(): jax.scipy.linalg.solve_triangular(diag_block, trailing[width:, :width].T,...]
    psum x0 -> x1, waiting for transfers between devices: none -> 94.7 us  [local(): right_t = lax.psum(right_t, 'member')]
    psum x1 -> x0, blocking collectives: 82.7 us -> none  [local(): reduced = lax.psum(partial_prod, 'tp').astype(jnp.bfloat16)]
    dot_general x15 -> x2, matrix products: 86.2 us -> 8.04 us  [mm(): return lax.dot_general(a, b, dims, preferred_element_type=f32)]
    reshape x4 -> x0, local copies, waits for them, and re-layouts: 76.8 us -> none  [the longest x2 54.8 us: local(): gram_total.transpose(1, 0, 2, 3).reshape(total_width, total_width)]
    another operation x98 -> x0, local copies, waits for them, and re-layouts: 65.1 us -> none  [the longest x66 49.1 us: block_solve(): jax.scipy.linalg.solve_triangular(factor[first:last, first:last], rhs_par...]
  transfers between devices with their start and end apart: 7 -> 6, of which waited for: 3 -> 4; matrix products, arithmetic and copies ran while one was open for 6% -> 5% of each run, Pallas kernels for 0% -> 0%
where the time goes in v1:
time: 729 us; the launch traced here: 728 us
  waiting for transfers between devices  376 us (52%)
  Pallas kernels  227 us (31%)
  blocking collectives  64 us (9%)
  local copies, waits for them, and re-layouts  30.8 us (4%)
  between operations  13.9 us (2%)
  starting transfers between devices  8.18 us (1%)
  matrix products  8.04 us (1%)
    pallas_call x1, Pallas kernels, factor_solve(): pl.pallas_call(factor_kernel, out_shape=jax.ShapeDtypeStruct((N, RC), bf1...  227 us
    all_gather x1, waiting for transfers between devices, local(): gram = lax.all_gather(share, ('tp', 'member'), axis=0, tiled=True)  212 us
    psum x1, waiting for transfers between devices, local(): right_t = lax.psum(right_t, 'member')  94.7 us
    all_gather x1, waiting for transfers between devices, local(): gathered = lax.all_gather(own, 'tp', axis=1, tiled=True)  63.8 us
    unnamed x1, blocking collectives  46.2 us
    unnamed x12, local copies, waits for them, and re-layouts  29.6 us
    all_to_all x1, blocking collectives, local(): lax.all_to_all(weights[0], 'tp', split_axis=1, concat_axis=0, tiled=True)  17.9 us
  transfers between devices with their start and end apart: 6, of which 4 were waited for; matrix products, arithmetic and copies ran while one was open for 5% of the time, Pallas kernels for 0%

profile of v1, /device:TPU:1, one launch (start us, length us, event | category | flops | bytes accessed | tf_op | source)
XLA Modules:
  0.0 727.9 jit_solution(8768195610133560744)
XLA Ops:
  6.5 0.7 all-gather.5.cloned.1.call-update
  7.3 0.0 all-gather.7.cloned.1.call-start
  7.3 63.8 %all-gather.5.cloned.1.call-done = bf16[1,512,2560]{1,2,0:T(8,128)(2,1)} async-done(((bf16[1,512,320]{1,2,0:T(8,128)(2,1)}), bf16[1,512,2560]{1,2,0:T(8,128)(2,1)}) %all-gather.5.cloned.1.call-update) | async-done | bytes 2621456 | tf_op jit(solution)/shard_map/all_gather | solution.py:201
  71.1 2.9 fusion.5
  74.0 46.2 %fusion = f32[24,2560]{1,0:T(8,128)S(1)} fusion(f32[320,2560]{1,0:T(8,128)S(1)} %fusion.5), kind=kCustom, calls=%all-reduce-scatter | all-reduce-scatter fusion | flops 983041 | bytes 3523072
  120.2 1.4 collective-permute-start.1
  121.6 5.4 collective-permute-start
  127.0 1.3 collective-permute-start.2
  128.3 0.6 dynamic-slice.4
  129.6 4.8 collective-permute-done.2
  134.4 0.7 concatenate
  135.1 0.7 dynamic-slice_bitcast_fusion
  135.8 0.0 all-gather.7.cloned.1.call-update
  135.8 0.0 all-reduce.4.cloned.1.call-start
  135.9 0.1 copy.9
  136.0 0.1 copy.7
  136.1 17.9 %all_to_all.19 = bf16[320,8,128]{2,0,1:T(8,128)(2,1)S(1)} all-to-all(bf16[320,8,128]{2,0,1:T(8,128)(2,1)S(1)} %copy.7), channel_id=1, replica_groups=mesh['member'=16,'tp'=8] {'tp'}, dimensions={1} | all-to-all | bytes 1310720 | tf_op jit(solution)/shard_map/all_to_all | solution.py:202
  154.0 1.1 copy.8
  155.1 0.6 multiply_reduce_fusion
  155.7 5.1 fusion.1
  160.8 211.6 %all-gather.7.cloned.1.call-done = f32[128,20,2560]{2,1,0:T(8,128)} async-done(((f32[1,20,2560]{2,1,0:T(8,128)}), f32[128,20,2560]{2,1,0:T(8,128)}) %all-gather.7.cloned.1.call-update) | async-done | bytes 26214416 | tf_op jit(solution)/shard_map/all_gather | solution.py:208
  372.4 27.5 %reshape.10.g_hbm = f32[2560,2560]{1,0:T(8,128)} reshape(f32[128,20,2560]{2,1,0:T(8,128)} %all-gather.7.cloned.1.call-done) | data formatting | bytes 52428800
  399.9 94.7 %all-reduce.4.cloned.1.call-done.r_ref = f32[128,2560]{1,0:T(8,128)} async-done(((f32[128,2560]{1,0:T(8,128)}), f32[128,2560]{1,0:T(8,128)}) %all-reduce.4.cloned.1.call-update) | async-done | bytes 1310736 | tf_op jit(solution)/shard_map/psum | solution.py:209
  494.6 226.7 %shard_map.28 = bf16[2560,128]{1,0:T(8,128)(2,1)} custom-call(f32[2560,2560]{1,0:T(8,128)} %reshape.10.g_hbm, f32[128,2560]{1,0:T(8,128)} %all-reduce.4.cloned.1.call-done.r_ref), custom_call_target="tpu_custom_call" | custom-call | tf_op jit(solution)/shard_map/pallas_call | solution.py:180
  (12 shorter events, 0.1 us)
Async XLA Ops:
  6.5 64.5 %all-gather.5.cloned.1.call-start = ((), (), s32[]{:S(2)}) async-start(), calls=%async_computation.2 | async-start | bytes 2949120 | tf_op jit(solution)/shard_map/all_gather | solution.py:201
  7.3 365.1 %all-gather.7.cloned.1.call-start = ((), (), s32[]{:S(2)}) async-start(), calls=%async_computation.3 | async-start | bytes 31703040 | tf_op jit(solution)/shard_map/all_gather | solution.py:208
  74.0 54.3 %copy-start.2 = (u32[128]{0:T(128)S(1)}, u32[128]{0:T(128)}, u32[]{:S(2)}) copy-start(u32[128]{0:T(128)} %constant.10) | copy-start | bytes 1540
  120.2 15.7 %copy-start.1 = (bf16[1,320,1024]{2,1,0:T(8,128)(2,1)S(1)}, bf16[1,320,1024]{2,1,0:T(8,128)(2,1)}, u32[]{:S(2)}) copy-start(bf16[1,320,1024]{2,1,0:T(8,128)(2,1)} %param.3) | copy-start | bytes 1966084
  120.2 14.2 %collective-permute-start.1 = (f32[24,2560]{1,0:T(8,128)S(1)}, f32[24,2560]{1,0:T(8,128)S(1)}, u32[]{:S(2)}, u32[]{:S(2)}) collective-permute-start(f32[24,2560]{1,0:T(8,128)S(1)} %fusion), channel_id=1, source_target_pairs={{0,16},{8,24},{16,32},{24,40},{32,48},{40,56},{48,64},{56,72},{64,... | collective-permute-start | bytes 737288
  121.6 12.8 %collective-permute-start = (f32[24,2560]{1,0:T(8,128)S(1)}, f32[24,2560]{1,0:T(8,128)S(1)}, u32[]{:S(2)}, u32[]{:S(2)}) collective-permute-start(f32[24,2560]{1,0:T(8,128)S(1)} %fusion), channel_id=1, source_target_pairs={{0,8},{8,16},{16,24},{24,32},{32,40},{40,48},{48,56},{56,64},{64,7... | collective-permute-start | bytes 737288
  127.0 7.4 %collective-permute-start.2 = (f32[12,2560]{1,0:T(8,128)S(1)}, f32[12,2560]{1,0:T(8,128)S(1)}, u32[]{:S(2)}, u32[]{:S(2)}) collective-permute-start(f32[12,2560]{1,0:T(8,128)S(1)} %slice), channel_id=1, source_target_pairs={{0,24},{8,32},{16,40},{24,48},{32,56},{40,64},{48,72},{56,80},{64,... | collective-permute-start | bytes 368648
  135.8 358.8 %all-reduce.4.cloned.1.call-start = ((), (), s32[]{:S(2)}) async-start(), calls=%async_computation.1 | async-start | bytes 2621440 | tf_op jit(solution)/shard_map/psum | solution.py:209
  135.9 19.2 %copy-start = (bf16[1,512,2560]{1,2,0:T(8,128)(2,1)S(1)}, bf16[1,512,2560]{1,2,0:T(8,128)(2,1)}, u32[]{:S(2)}) copy-start(bf16[1,512,2560]{1,2,0:T(8,128)(2,1)} %all-gather.5.cloned.1.call-done) | copy-start | bytes 7864324
Sparse Core Ops, SparseCore 0:
  9.7 61.3 all-gather.4
  135.9 236.4 all-gather.6
  374.9 119.6 all-reduce.3

commit v2 on v1

--- a/solution.py
+++ b/solution.py
@@ -11,7 +11,6 @@
 H = 128
 NT = (((1,), (1,)), ((), ()))
 NN = (((1,), (0,)), ((), ()))
-TN = (((0,), (0,)), ((), ()))
 
 
 def split(x):
@@ -77,27 +76,352 @@
                 a[g] = new
     return jnp.concatenate(out, 0)
 
+MESH = pl.DeviceIdType.MESH
+TN = (((0,), (0,)), ((), ()))
+NS = 7
+PARTS = ((0, 2), (2, 2), (4, 3))
+
+
+def place():
+    m = lax.axis_index("member")
+    t = lax.axis_index("tp")
+    x = (t // 4) * 2 + (m // 2) % 2
+    return x, m // 4, t % 4, m % 2
+
+
+def device(x, y, z, c):
+    return ((y * 2 + x % 2) * 2 + c, (x // 2) * 4 + z)
+
+
+def greet(peers):
+    barrier = pltpu.get_barrier_semaphore()
+    for peer in peers:
+        pl.semaphore_signal(barrier, inc=1, device_id=peer, device_id_type=MESH)
+    pl.semaphore_wait(barrier, len(peers))
+
+
+def remote(src, dst, send, recv, peer):
+    return pltpu.make_async_remote_copy(
+        src_ref=src, dst_ref=dst, send_sem=send, recv_sem=recv, device_id=peer, device_id_type=MESH
+    )
+
+
+def gather_kernel(a_ref, w_ref, at_ref, wc_ref, wx, send, recv, own):
+    x, y, z, c = place()
+    xh = x // 2
+    t = xh * 4 + z
+    other = (1 - xh) * 4 + z
+    half = a_ref.shape[0] // 2
+    partner = device((x + 2) % 4, y, z, c)
+    ring = [device(x, y, (z + d) % 4, c) for d in range(4)]
+    greet([partner] + ring[1:])
+
+    def copy(i, src, dst, peer):
+        made = remote(src, dst, send.at[i], recv.at[i], peer)
+        made.start()
+        return made
+
+    def cols(first):
+        return pl.ds(pl.multiple_of(first * 128, 128), 128)
+
+    copies = {}
+    copies[0] = copy(0, a_ref, at_ref.at[t], partner)
+    copies[1] = copy(1, a_ref, at_ref.at[t], ring[1])
+    copies[2] = copy(2, a_ref, at_ref.at[t], ring[3])
+    far = pl.ds(pl.multiple_of((1 - xh) * 512, 512), 512)
+    copies[9] = copy(9, w_ref.at[:, far], wx, partner)
+    for d in range(1, 4):
+        src = w_ref.at[:, cols(xh * 4 + (z + d) % 4)]
+        copies[9 + d] = copy(9 + d, src, wc_ref.at[t], ring[d])
+    keep_a = pltpu.make_async_copy(a_ref, at_ref.at[t], own.at[0])
+    keep_a.start()
+    keep_w = pltpu.make_async_copy(w_ref.at[:, cols(t)], wc_ref.at[t], own.at[1])
+    keep_w.start()
+    copies[0].wait_recv()
+    copies[3] = copy(3, at_ref.at[other], at_ref.at[other], ring[1])
+    copies[4] = copy(4, at_ref.at[other], at_ref.at[other], ring[3])
+    for at, side in ((0, xh), (2, 1 - xh)):
+        before = side * 4 + (z + 3) % 4
+        after = side * 4 + (z + 1) % 4
+        copies[1 + at].wait_recv()
+        part = at_ref.at[before, pl.ds(0, half)]
+        copies[5 + at] = copy(5 + at, part, part, ring[1])
+        copies[2 + at].wait_recv()
+        part = at_ref.at[after, pl.ds(half, half)]
+        copies[6 + at] = copy(6 + at, part, part, ring[3])
+    copies[9].wait_recv()
+    keep_x = pltpu.make_async_copy(wx.at[:, cols(z)], wc_ref.at[other], own.at[2])
+    keep_x.start()
+    for d in range(1, 4):
+        src = wx.at[:, cols((z + d) % 4)]
+        copies[12 + d] = copy(12 + d, src, wc_ref.at[other], ring[d])
+    for i in (5, 6, 7, 8, 10, 11, 12, 13, 14, 15):
+        copies[i].wait_recv()
+    for i in range(16):
+        copies[i].wait_send()
+    keep_a.wait()
+    keep_w.wait()
+    keep_x.wait()
+
+
+def gather_acts(acts_t, weight):
+    width, rows = acts_t.shape
+    vmem = pl.BlockSpec(memory_space=pltpu.VMEM)
+    return pl.pallas_call(
+        gather_kernel,
+        out_shape=(
+            jax.ShapeDtypeStruct((8, width, rows), bf16),
+            jax.ShapeDtypeStruct((8, width, 128), bf16),
+        ),
+        in_specs=[vmem, vmem],
+        out_specs=(vmem, vmem),
+        scratch_shapes=[
+            pltpu.VMEM((width, 512), bf16),
+            pltpu.SemaphoreType.DMA((16,)),
+            pltpu.SemaphoreType.DMA((16,)),
+            pltpu.SemaphoreType.DMA((3,)),
+        ],
+        compiler_params=pltpu.CompilerParams(
+            collective_id=0, has_side_effects=True, vmem_limit_bytes=32 * 1024 * 1024
+        ),
+    )(acts_t, weight)
+
+
+def product_kernel(at_ref, wc_ref, part_ref, right_ref):
+    t = lax.axis_index("tp")
+    projected = mm(at_ref[...], wc_ref[...], TN).astype(bf16)
+    for i in range(10):
+        rows = pl.ds(i * 256, 256)
+        own = at_ref[rows, :]
+        wide = own.astype(f32)
+        diag = jnp.sum(wide * wide, axis=1, keepdims=True)
+        scaled = diag * wc_ref[rows, :].astype(f32)
+        right_ref[rows, :] = SHRINK * mm(own, projected) + (1.0 - SHRINK) * scaled
+    for s in range(NS):
+        b = jnp.minimum(s * 8 + t, 54)
+        k = 0
+        for j in range(1, 10):
+            k = k + (b >= 10 * j - j * (j - 1) // 2).astype(jnp.int32)
+        i = b - (10 * k - k * (k - 1) // 2) + k
+        left = at_ref[pl.ds(pl.multiple_of(i * 256, 256), 256), :]
+        right = at_ref[pl.ds(pl.multiple_of(k * 256, 256), 256), :]
+        part_ref[s] = mm(left, right, NT)
+
+
+def products(at, wc):
+    vmem = pl.BlockSpec(memory_space=pltpu.VMEM)
+    return pl.pallas_call(
+        product_kernel,
+        out_shape=(
+            jax.ShapeDtypeStruct((NS, 256, 256), f32),
+            jax.ShapeDtypeStruct((2560, 128), f32),
+        ),
+        in_specs=[vmem, vmem],
+        out_specs=(vmem, vmem),
+        compiler_params=pltpu.CompilerParams(vmem_limit_bytes=40 * 1024 * 1024),
+    )(at, wc)
+
+
+def sum_kernel(g_ref, r_ref, go_ref, ro_ref, g_pair, r_pair, g_in, r_in, send, recv):
+    x, y, z, c = place()
+    q = (x % 2) * 4 + y
+    pair = device(x, y, z, 1 - c)
+    peers = []
+    for d in range(1, 8):
+        p = (q + d) % 8
+        peers.append((p, device((x // 2) * 2 + p // 4, p % 4, z, c)))
+    greet([pair] + [device_id for _, device_id in peers])
+    first = [
+        remote(g_ref.at[:, 1 - c], g_pair, send.at[0], recv.at[0], pair),
+        remote(r_ref.at[1 - c], r_pair, send.at[1], recv.at[1], pair),
+    ]
+    for copy in first:
+        copy.start()
+    for copy in first:
+        copy.wait_recv()
+    g_pair[...] = g_pair[...] + g_ref[:, c]
+    r_pair[...] = r_pair[...] + r_ref[c]
+    second = []
+    for d, (p, peer) in enumerate(peers):
+        second.append(remote(g_pair.at[:, p], g_in.at[d], send.at[2 + d], recv.at[2 + d], peer))
+        second.append(remote(r_pair.at[p], r_in.at[d], send.at[9 + d], recv.at[9 + d], peer))
+    for copy in second:
+        copy.start()
+    for copy in second:
+        copy.wait_recv()
+    g_sum = g_pair[:, q]
+    r_sum = r_pair[q]
+    for d in range(7):
+        g_sum = g_sum + g_in[d]
+        r_sum = r_sum + r_in[d]
+    go_ref[...] = g_sum
+    ro_ref[...] = r_sum
+    for copy in first + second:
+        copy.wait_send()
+
+
+def sum_members(part, right):
+    vmem = pl.BlockSpec(memory_space=pltpu.VMEM)
+    return pl.pallas_call(
+        sum_kernel,
+        out_shape=(
+            jax.ShapeDtypeStruct((NS, 16, 256), f32),
+            jax.ShapeDtypeStruct((160, 128), f32),
+        ),
+        in_specs=[vmem, vmem],
+        out_specs=(vmem, vmem),
+        scratch_shapes=[
+            pltpu.VMEM((NS, 8, 16, 256), f32),
+            pltpu.VMEM((8, 160, 128), f32),
+            pltpu.VMEM((7, NS, 16, 256), f32),
+            pltpu.VMEM((7, 160, 128), f32),
+            pltpu.SemaphoreType.DMA((16,)),
+            pltpu.SemaphoreType.DMA((16,)),
+        ],
+        compiler_params=pltpu.CompilerParams(
+            collective_id=1, has_side_effects=True, vmem_limit_bytes=40 * 1024 * 1024
+        ),
+    )(part.reshape(NS, 2, 8, 16, 256), right.reshape(2, 8, 160, 128))
+
+
+def spread_kernel(g_ref, r_ref, go_ref, ro_ref, send, recv, rsend, rrecv, own):
+    x, y, z, c = place()
+    coord = (x, y, z)
+    q = (x % 2) * 4 + y
+    pair = device(x, y, z, 1 - c)
+    peers = []
+    for d in range(1, 8):
+        p = (q + d) % 8
+        peers.append(device((x // 2) * 2 + p // 4, p % 4, z, c))
+
+    def along(axis, shift):
+        moved = list(coord)
+        moved[axis] = (moved[axis] + shift) % 4
+        return device(*moved, c)
+
+    ring = [(along(axis, 1), along(axis, 3)) for axis in range(3)]
+    greet([pair] + peers + [one for both in ring for one in both])
+
+    keep_g = pltpu.make_async_copy(g_ref, go_ref.at[:, c, x, y, z], own.at[0])
+    keep_r = pltpu.make_async_copy(r_ref, ro_ref.at[c * 8 + q], own.at[1])
+    keep_g.start()
+    keep_r.start()
+    keep_g.wait()
+    keep_r.wait()
+
+    def view(p, phase, value, rows=None):
+        order = (p, (p + 1) % 3, (p + 2) % 3)
+        index = list(coord)
+        for axis in order[:phase]:
+            index[axis] = pl.ds(0, 4)
+        index[order[phase]] = value
+        first, count = PARTS[p]
+        index = [pl.ds(first, count), c] + index
+        if rows is not None:
+            index.append(pl.ds(rows, 8))
+        return go_ref.at[tuple(index)]
+
+    started = []
+
+    def copy(ref, sems, i, peer):
+        made = remote(ref, ref, sems[0].at[i], sems[1].at[i], peer)
+        made.start()
+        started.append(made)
+        return made
+
+    g_sems, r_sems = (send, recv), (rsend, rrecv)
+    r_copies = [copy(ro_ref.at[c * 8 + q], r_sems, d, peer) for d, peer in enumerate(peers)]
+    last = []
+    for phase in range(3):
+        first = {}
+        second = {}
+        for p in range(3):
+            axis = (p + phase) % 3
+            mine = view(p, phase, coord[axis])
+            base = (p * 3 + phase) * 4
+            first[p] = (copy(mine, g_sems, base, ring[axis][0]), copy(mine, g_sems, base + 1, ring[axis][1]))
+            if phase == 2:
+                last.append(copy(mine, g_sems, 36 + p * 4, pair))
+        for p in range(3):
+            axis = (p + phase) % 3
+            base = (p * 3 + phase) * 4
+            before, after = (coord[axis] + 3) % 4, (coord[axis] + 1) % 4
+            first[p][0].wait_recv()
+            one = copy(view(p, phase, before, 0), g_sems, base + 2, ring[axis][0])
+            first[p][1].wait_recv()
+            two = copy(view(p, phase, after, 8), g_sems, base + 3, ring[axis][1])
+            second[p] = (one, two)
+            if phase == 2:
+                last.append(copy(view(p, phase, before), g_sems, 37 + p * 4, pair))
+                last.append(copy(view(p, phase, after), g_sems, 38 + p * 4, pair))
+        if phase == 0:
+            for made in r_copies:
+                made.wait_recv()
+            last.append(copy(ro_ref.at[pl.ds(pl.multiple_of(c * 8, 8), 8)], r_sems, 7, pair))
+        for p in range(3):
+            axis = (p + phase) % 3
+            second[p][0].wait_recv()
+            second[p][1].wait_recv()
+            if phase == 2:
+                far = (coord[axis] + 2) % 4
+                last.append(copy(view(p, phase, far), g_sems, 39 + p * 4, pair))
+    for made in last:
+        made.wait_recv()
+    for made in started:
+        made.wait_send()
+
+
+def spread(gram, right):
+    hbm = pl.BlockSpec(memory_space=pl.ANY)
+    vmem = pl.BlockSpec(memory_space=pltpu.VMEM)
+    return pl.pallas_call(
+        spread_kernel,
+        out_shape=(
+            jax.ShapeDtypeStruct((NS, 2, 4, 4, 4, 16, 256), f32),
+            jax.ShapeDtypeStruct((16, 160, 128), f32),
+        ),
+        in_specs=[vmem, vmem],
+        out_specs=(hbm, hbm),
+        scratch_shapes=[
+            pltpu.SemaphoreType.DMA((48,)),
+            pltpu.SemaphoreType.DMA((48,)),
+            pltpu.SemaphoreType.DMA((8,)),
+            pltpu.SemaphoreType.DMA((8,)),
+            pltpu.SemaphoreType.DMA((2,)),
+        ],
+        compiler_params=pltpu.CompilerParams(collective_id=2, has_side_effects=True),
+    )(gram, right)
+
 N = 2560
 NB = N // B
 RC = 128
 
 
 def factor_kernel(g_hbm, r_ref, o_ref, panel, low, y_low, y, x_low, w_low, acc, sems):
+    def block(k, i, slot):
+        b = 10 * k - k * (k - 1) // 2 + i - k
+        s, t = b // 8, b % 8
+        src = g_hbm.at[s, :, pl.ds((t // 4) * 2, 2), :, t % 4]
+        return pltpu.make_async_copy(src, panel.at[slot, i], sems.at[slot, i])
+
     def fetch(k, slot):
-        cols = pl.ds(pl.multiple_of(k * B, B), B)
-        return pltpu.make_async_copy(g_hbm.at[:, cols], panel.at[slot], sems.at[slot])
-
-    fetch(0, 0).start()
+        def one(i, _):
+            block(k, i, slot).start()
+            return 0
+
+        lax.fori_loop(k, NB, one, 0)
+
+    fetch(0, 0)
     row = lax.broadcasted_iota(jnp.int32, (B, B), 0)
     col = lax.broadcasted_iota(jnp.int32, (B, B), 1)
 
     def step(k, _):
-        slot = lax.rem(k, 2)
-        fetch(k, slot).wait()
+        slot = k % 2
+        block(k, k, slot).wait()
 
         @pl.when(k + 1 < NB)
         def _():
-            fetch(k + 1, 1 - slot).start()
+            fetch(k + 1, 1 - slot)
 
         own_cols = pl.ds(pl.multiple_of(k * B, B), B)
 
@@ -112,7 +436,7 @@
 
             lax.fori_loop(0, k, one, 0)
 
-        tile = panel[slot, own_cols, :]
+        tile = panel[slot, k].reshape(B, B)
         acc[...] = jnp.where(row == col, tile, SHRINK * tile)
         subtract(low.at[k], B, pl.ds(0, B))
         w1 = inverse_factor(acc[:H, :H])
@@ -131,7 +455,8 @@
             return mm(ch, wh, NT) + (mm(ch, w_low[k, B:, :], NT) + mm(cl, wh, NT))
 
         def below(i, _):
-            acc[...] = SHRINK * panel[slot, pl.ds(pl.multiple_of(i * B, B), B), :]
+            block(k, i, slot).wait()
+            acc[...] = SHRINK * panel[slot, i].reshape(B, B)
             subtract(low.at[i], B, pl.ds(0, B))
             h, l = split(scale(acc[...]))
             low[i, :B, own_cols] = h
@@ -139,7 +464,7 @@
             return 0
 
         lax.fori_loop(k + 1, NB, below, 0)
-        acc[:RC, :] = r_ref[:, own_cols]
+        acc[:RC, :] = r_ref[own_cols, :].T
         subtract(y_low, RC, pl.ds(0, RC))
         yk = scale(acc[:RC, :])
         y[:, own_cols] = yk
@@ -176,38 +501,31 @@
     lax.fori_loop(0, NB, back, 0)
 
 
-def factor_solve(gram, right_t):
+def factor_solve(gram, right):
     return pl.pallas_call(
         factor_kernel,
         out_shape=jax.ShapeDtypeStruct((N, RC), bf16),
         in_specs=[pl.BlockSpec(memory_space=pl.ANY), pl.BlockSpec(memory_space=pltpu.VMEM)],
         out_specs=pl.BlockSpec(memory_space=pltpu.VMEM),
         scratch_shapes=[
-            pltpu.VMEM((2, N, B), f32),
+            pltpu.VMEM((2, NB, 2, 2, 4, 16, 256), f32),
             pltpu.VMEM((NB, 2 * B, N), bf16),
             pltpu.VMEM((2 * RC, N), bf16),
             pltpu.VMEM((RC, N), f32),
             pltpu.VMEM((2 * RC, N), bf16),
             pltpu.VMEM((NB, 2 * B, B), bf16),
             pltpu.VMEM((B, B), f32),
-            pltpu.SemaphoreType.DMA((2,)),
+            pltpu.SemaphoreType.DMA((2, NB)),
         ],
         compiler_params=pltpu.CompilerParams(vmem_limit_bytes=56 * 1024 * 1024),
-    )(gram, right_t)
+    )(gram, right)
 
 
 def local(acts, weights):
-    own = acts[0]
-    gathered = lax.all_gather(own, "tp", axis=1, tiled=True)
-    columns = lax.all_to_all(weights[0], "tp", split_axis=1, concat_axis=0, tiled=True)
-    projected = mm(gathered, columns).astype(bf16)
-    diag = jnp.sum(jnp.square(gathered.astype(f32)), axis=0)
-    right_t = SHRINK * mm(projected, gathered, TN)
-    right_t = right_t + (1.0 - SHRINK) * diag[None, :] * columns.T.astype(f32)
-    share = lax.psum_scatter(mm(own, gathered, TN), "member", scatter_dimension=0, tiled=True)
-    gram = lax.all_gather(share, ("tp", "member"), axis=0, tiled=True)
-    right_t = lax.psum(right_t, "member")
-    return factor_solve(gram, right_t)
+    at, wc = gather_acts(acts[0].T, weights[0])
+    part, right = products(at.reshape(N, -1), wc.reshape(N, RC))
+    gram, right = spread(*sum_members(part, right))
+    return factor_solve(gram, right.reshape(N, RC))
 
 
 def solution(mesh):

time: 729 us -> 359 us (0.49)
  waiting for transfers between devices: 376 us -> 0 us
  Pallas kernels: 227 us -> 355 us
  blocking collectives: 64 us -> 0 us
  local copies, waits for them, and re-layouts: 30.8 us -> 3.32 us
  between operations: 13.9 us -> 0.2 us
  starting transfers between devices: 8.18 us -> 0 us
  matrix products: 8.04 us -> 0 us
    all_gather x2 -> x0, waiting for transfers between devices: 275 us -> none  [the longest x1 212 us: local(): gram = lax.all_gather(share, ('tp', 'member'), axis=0, tiled=True)]
    pallas_call x0 -> x4, Pallas kernels: none -> 127 us  [the longest x1 60.6 us: spread(): pl.pallas_call(spread_kernel, out_shape=(jax.ShapeDtypeStruct((NS, 2, 4,...]
    psum x1 -> x0, waiting for transfers between devices: 94.7 us -> none  [local(): right_t = lax.psum(right_t, 'member')]
    unnamed x1 -> x0, blocking collectives: 46.2 us -> none
    unnamed x12 -> x8, local copies, waits for them, and re-layouts: 29.6 us -> 3.32 us
    all_to_all x1 -> x0, blocking collectives: 17.9 us -> none  [local(): lax.all_to_all(weights[0], 'tp', split_axis=1, concat_axis=0, tiled=True)]
    unnamed x3 -> x0, starting transfers between devices: 8.09 us -> none
    dot_general x2 -> x0, matrix products: 8.04 us -> none  [mm(): return lax.dot_general(a, b, dims, preferred_element_type=f32)]
  transfers between devices with their start and end apart: 6 -> 0, of which waited for: 4 -> 0; matrix products, arithmetic and copies ran while one was open for 5% -> 0% of each run, Pallas kernels for 0% -> 0%
where the time goes in v2:
time: 359 us
  Pallas kernels  355 us (99%)
    pallas_call x1, Pallas kernels, factor_solve(): pl.pallas_call(factor_kernel, out_shape=jax.ShapeDtypeStruct((N, RC), bf1...  228 us
    pallas_call x1, Pallas kernels, spread(): pl.pallas_call(spread_kernel, out_shape=(jax.ShapeDtypeStruct((NS, 2, 4,...  60.6 us
    pallas_call x1, Pallas kernels, gather_acts(): pl.pallas_call(gather_kernel, out_shape=(jax.ShapeDtypeStruct((8, width,...  35.4 us
    pallas_call x1, Pallas kernels, sum_members(): pl.pallas_call(sum_kernel, out_shape=(jax.ShapeDtypeStruct((NS, 16, 256),...  27.1 us

profile of v2, /device:TPU:1, one launch (start us, length us, event | category | flops | bytes accessed | tf_op | source)
XLA Modules:
  0.0 358.6 jit_solution(16348708682076064340)
XLA Ops:
  0.0 0.0 copy-start
  0.0 1.1 copy-done
  1.1 0.0 copy-start.1
  1.1 1.0 copy-done.1
  2.1 35.4 %shard_map.28 = (bf16[8,320,512]{2,1,0:T(8,128)(2,1)S(1)}, bf16[8,320,128]{2,1,0:T(8,128)(2,1)S(1)}) custom-call(bf16[320,512]{1,0:T(8,128)(2,1)S(1)} %bitcast.14, bf16[320,1024]{1,0:T(8,128)(2,1)S(1)} %bitcast.12), custom_call_target="tpu_custom_call" | custom-call | tf_op jit(solution)/shard_map/pallas_call | solution.py:170
  37.5 3.5 shard_map.29
  40.9 27.1 %shard_map.30 = (f32[7,16,256]{2,1,0:T(8,128)S(1)}, f32[160,128]{1,0:T(8,128)S(1)}) custom-call(f32[7,2,8,16,256]{4,3,2,1,0:T(8,128)S(1)} %bitcast.10, f32[2,8,160,128]{3,2,1,0:T(8,128)S(1)} %bitcast.11), custom_call_target="tpu_custom_call" | custom-call | tf_op jit(solution)/shard_map/pallas_call | solution.py:265
  68.1 0.0 copy-start.2
  68.1 0.6 copy-done.2
  68.7 0.0 copy-start.3
  68.7 0.6 copy-done.3
  69.3 60.6 %shard_map.31 = (f32[7,2,4,4,4,16,256]{6,5,4,3,2,1,0:T(8,128)}, f32[16,160,128]{2,1,0:T(8,128)}) custom-call(f32[7,16,256]{2,1,0:T(8,128)} %copy-done.2, f32[160,128]{1,0:T(8,128)} %copy-done.3), custom_call_target="tpu_custom_call" | custom-call | tf_op jit(solution)/shard_map/pallas_call | solution.py:377
  130.0 228.5 %shard_map.32 = bf16[2560,128]{1,0:T(8,128)(2,1)} custom-call(f32[7,2,4,4,4,16,256]{6,5,4,3,2,1,0:T(8,128)} %get-tuple-element.19.g_hbm, f32[2560,128]{1,0:T(8,128)} %bitcast.15), custom_call_target="tpu_custom_call" | custom-call | tf_op jit(solution)/shard_map/pallas_call | solution.py:505
Async XLA Ops:
  0.0 1.1 copy-start
  1.1 1.0 copy-start.1
  68.1 0.6 copy-start.2
  68.7 0.6 copy-start.3
